TPU v7x, 32 devices: a whole 2x2x4 slice. The times are simulated.
32 devices in a mesh: tm: 2 (over x), gz: 4 (over y, core), view: 4 (over z).
Axes of the slice: x: 2, y: 2, z: 4, core: 2. Of those that a mesh axis runs over, the one named last changes fastest.
Arguments:
- sinogram: bfloat16 [2, 8, 512, 2560], P(None, 'view', ('tm', 'gz')), may hold values from 102 to 358
- projector: bfloat16 [8, 1024, 2560], P('view'), may hold values from 0.0099487305 to 1
- warm_volume: float32 [512, 1024], P(('tm', 'gz')), may hold values from 0.2 to 2.5, as said below
- view_order: int32 [2], replicated, may hold values from 0 to 1, each once
Outputs:
- volumes: float32 [2, 512, 1024], P(None, ('tm', 'gz'))
Inputs may be any that keep to these rules, and one draw needn't show every extreme that they name: `view_order`: each local view number appears once. `warm_volume`: positive attenuation values.
All inputs are finite; a program needn't handle non-finite values.
Results may differ from a plain program's by a relative error of at most 0.0003.
Values may be sent and summed in bfloat16 or wider, within the bound.
A program may use at most 64 MiB of HBM per device.

v0:
```python
import jax
import jax.numpy as jnp
from jax import lax
from jax.sharding import PartitionSpec as P

RY = 128
FRAMES = 2
SWEEPS = 3
TV_STEPS = 2


RELAXATION = 0.9
STEP_SCALE = 0.3
STEP_DECAY = 0.7
SMOOTHING = 0.01
NORM_GUARD = 1e-06


def padded(block, sides, width):
    for axis, dim in sides:
        count = lax.axis_size(axis)
        forward = [(i, i + 1) for i in range(count - 1)]
        backward = [(target, source) for source, target in forward]
        low = lax.ppermute(
            lax.slice_in_dim(block, block.shape[dim] - width, None, axis=dim), axis, forward
        )
        high = lax.ppermute(lax.slice_in_dim(block, 0, width, axis=dim), axis, backward)
        block = jnp.concatenate([low, block, high], axis=dim)
    return block


def tv_gradient(volume, first_z, depth_total):
    row_count = volume.shape[0]
    pixels = volume.shape[1]
    zero_row = jnp.zeros((1, pixels), jnp.float32)
    zero_band = jnp.zeros((row_count, RY), jnp.float32)
    zero_col = jnp.zeros((row_count, 1), jnp.float32)
    zindex = first_z + jnp.arange(row_count, dtype=jnp.int32)
    inside = ((zindex >= 0) & (zindex < depth_total - 1)).astype(jnp.float32)
    diff_z = jnp.concatenate([volume[1:] - volume[:-1], zero_row], axis=0) * inside[:, None]
    diff_i = jnp.concatenate([volume[:, RY:] - volume[:, :-RY], zero_band], axis=1)
    column = jnp.arange(pixels, dtype=jnp.int32) % RY
    diff_j = jnp.concatenate([volume[:, 1:] - volume[:, :-1], zero_col], axis=1)
    diff_j = diff_j * (column < RY - 1).astype(jnp.float32)[None, :]
    magnitude = jnp.sqrt(diff_z * diff_z + diff_i * diff_i + diff_j * diff_j + SMOOTHING)
    flux_z = diff_z / magnitude
    flux_i = diff_i / magnitude
    flux_j = diff_j / magnitude
    gradient = jnp.concatenate([zero_row, flux_z[:-1]], axis=0) - flux_z
    gradient = gradient + (jnp.concatenate([zero_band, flux_i[:, :-RY]], axis=1) - flux_i)
    gradient = gradient + (jnp.concatenate([zero_col, flux_j[:, :-1]], axis=1) - flux_j)
    return gradient


def body(sinogram, projector, warm_volume, view_order):
    slices = warm_volume.shape[0]
    pixels = warm_volume.shape[1]
    per_view = projector.shape[0]
    ray_sums = jnp.sum(projector, axis=1, dtype=jnp.float32)
    coverage = lax.psum(jnp.sum(projector, axis=2, dtype=jnp.float32), "view")
    slab_count = lax.axis_size("tm") * lax.axis_size("gz")
    slab_index = lax.axis_index("tm") * lax.axis_size("gz") + lax.axis_index("gz")
    depth_total = slices * slab_count
    cell_count = depth_total * pixels
    rim_width = 1

    def make_project(measured, slot_index):
        ray_tile = lax.dynamic_index_in_dim(projector, slot_index, 0, keepdims=False)
        ray_total = lax.dynamic_index_in_dim(ray_sums, slot_index, 0, keepdims=False)
        observed = lax.dynamic_index_in_dim(measured, slot_index, 0, keepdims=False)

        def project(piece_rows, first_row):
            forward = jnp.dot(piece_rows, ray_tile, preferred_element_type=jnp.float32)
            mismatch = ((observed.astype(jnp.float32) - forward) / ray_total[None, :]).astype(
                jnp.bfloat16
            )
            return lax.dot_general(
                mismatch, ray_tile, (((1,), (1,)), ((), ())), preferred_element_type=jnp.float32
            )

        return project

    first_slice = slab_index * slices
    current = warm_volume
    finished = []
    for frame_no in range(FRAMES):
        reconstruct_current = current
        reconstruct_measured = sinogram[frame_no]
        for sweep_no in range(SWEEPS):
            superize_current = reconstruct_current
            first_step = sweep_no * TV_STEPS
            for step_no in range(TV_STEPS):
                extended = padded(superize_current, ((("tm", "gz"), 0),), rim_width)
                gradient = tv_gradient(extended, first_slice - 1, depth_total)[1:-1]
                spread = jnp.sqrt(
                    lax.psum(jnp.sum(gradient * gradient), ("tm", "gz")) / cell_count + NORM_GUARD
                )
                superize_current = (
                    superize_current
                    - STEP_SCALE * STEP_DECAY ** (first_step + step_no) * gradient / spread
                )
            reconstruct_current = superize_current
            for subset in range(per_view):
                reconstruct_slot_index = view_order[subset]
                reconstruct_project = make_project(reconstruct_measured, reconstruct_slot_index)
                partial_back = reconstruct_project(reconstruct_current.astype(jnp.bfloat16), 0)
                summed = lax.psum(partial_back, "view")
                weight = lax.dynamic_index_in_dim(
                    coverage, reconstruct_slot_index, 0, keepdims=False
                )
                reconstruct_current = jnp.maximum(
                    reconstruct_current + RELAXATION * summed / weight[None, :], 0.0
                )
        current = reconstruct_current
        finished.append(current)
    volumes = jnp.stack(finished, axis=0)
    return volumes


def solution(mesh):
    return jax.shard_map(
        body,
        mesh=mesh,
        in_specs=(
            P(None, "view", ("tm", "gz"), None),
            P("view", None, None),
            P(("tm", "gz"), None),
            P(),
        ),
        out_specs=P(None, ("tm", "gz"), None),
        check_vma=False,
    )
```

profile of v0, /device:TPU:25, one launch (start us, length us, event | category | flops | bytes accessed | tf_op | source)
XLA Modules:
  0.0 834.6 jit_solution(13394525069003305715)
XLA Ops:
  7.4 3.7 collective-permute-start.1
  13.1 7.5 convert_reduce_fusion
  22.1 12.3 %psum.175 = f32[]{:T(128)} all-reduce(f32[]{:T(128)} %get-tuple-element.31), channel_id=1, replica_groups=mesh['tm'=2,'gz'=4,'view'=4] {'tm','gz'}, use_global_device_ids=true, to_apply=%region_1.0 | all-reduce | flops 1 | bytes 8 | tf_op jit(solution)/shard_map/psum | solution.py:96
  35.1 2.5 collective-permute-start.3
  37.6 2.3 collective-permute-start.2
  45.9 12.4 %psum.176 = f32[]{:T(128)} all-reduce(f32[]{:T(128)} %get-tuple-element.29), channel_id=1, replica_groups=mesh['tm'=2,'gz'=4,'view'=4] {'tm','gz'}, use_global_device_ids=true, to_apply=%region_3.4 | all-reduce | flops 1 | bytes 8 | tf_op jit(solution)/shard_map/psum | solution.py:96
  59.0 7.4 fusion.44
  66.5 6.5 psum.178
  73.0 28.6 %all-reduce.85.cloned.1.call-done = f32[64,1024]{1,0:T(8,128)} async-done(((f32[64,1024]{1,0:T(8,128)}), f32[64,1024]{1,0:T(8,128)}) %all-reduce.85.cloned.1.call-update) | async-done | bytes 262160 | tf_op jit(solution)/shard_map/psum | solution.py:107
  102.7 7.4 fusion.20
  110.1 35.2 %all-reduce.87.cloned.1.call-done = f32[64,1024]{1,0:T(8,128)} async-done(((f32[64,1024]{1,0:T(8,128)}), f32[64,1024]{1,0:T(8,128)}) %all-reduce.87.cloned.1.call-update) | async-done | bytes 262160 | tf_op jit(solution)/shard_map/psum | solution.py:107
  146.3 5.5 collective-permute-start.5
  153.8 3.0 collective-permute-done.4
  158.1 11.1 %psum.180 = f32[]{:T(128)} all-reduce(f32[]{:T(128)} %get-tuple-element.27), channel_id=1, replica_groups=mesh['tm'=2,'gz'=4,'view'=4] {'tm','gz'}, use_global_device_ids=true, to_apply=%region_10.11 | all-reduce | flops 1 | bytes 8 | tf_op jit(solution)/shard_map/psum | solution.py:96
  169.9 4.2 collective-permute-start.7
  174.1 1.9 collective-permute-start.6
  176.0 3.0 collective-permute-done.6
  180.4 13.7 %psum.181 = f32[]{:T(128)} all-reduce(f32[]{:T(128)} %get-tuple-element.25), channel_id=1, replica_groups=mesh['tm'=2,'gz'=4,'view'=4] {'tm','gz'}, use_global_device_ids=true, to_apply=%region_12.13 | all-reduce | flops 1 | bytes 8 | tf_op jit(solution)/shard_map/psum | solution.py:96
  194.7 7.4 fusion.40
  202.4 35.4 %all-reduce.89.cloned.1.call-done = f32[64,1024]{1,0:T(8,128)} async-done(((f32[64,1024]{1,0:T(8,128)}), f32[64,1024]{1,0:T(8,128)}) %all-reduce.89.cloned.1.call-update) | async-done | bytes 262160 | tf_op jit(solution)/shard_map/psum | solution.py:107
  238.8 7.4 fusion.16
  246.2 35.2 %all-reduce.91.cloned.1.call-done = f32[64,1024]{1,0:T(8,128)} async-done(((f32[64,1024]{1,0:T(8,128)}), f32[64,1024]{1,0:T(8,128)}) %all-reduce.91.cloned.1.call-update) | async-done | bytes 262160 | tf_op jit(solution)/shard_map/psum | solution.py:107
  282.4 5.5 collective-permute-start.9
  289.9 3.0 collective-permute-done.8
  294.2 11.1 %psum.184 = f32[]{:T(128)} all-reduce(f32[]{:T(128)} %get-tuple-element.23), channel_id=1, replica_groups=mesh['tm'=2,'gz'=4,'view'=4] {'tm','gz'}, use_global_device_ids=true, to_apply=%region_16.17 | all-reduce | flops 1 | bytes 8 | tf_op jit(solution)/shard_map/psum | solution.py:96
  306.0 4.2 collective-permute-start.11
  310.2 1.9 collective-permute-start.10
  312.2 3.0 collective-permute-done.10
  316.5 13.7 %psum.185 = f32[]{:T(128)} all-reduce(f32[]{:T(128)} %get-tuple-element.21), channel_id=1, replica_groups=mesh['tm'=2,'gz'=4,'view'=4] {'tm','gz'}, use_global_device_ids=true, to_apply=%region_18.19 | all-reduce | flops 1 | bytes 8 | tf_op jit(solution)/shard_map/psum | solution.py:96
  330.9 7.4 fusion.36
  338.3 35.5 %all-reduce.93.cloned.1.call-done = f32[64,1024]{1,0:T(8,128)} async-done(((f32[64,1024]{1,0:T(8,128)}), f32[64,1024]{1,0:T(8,128)}) %all-reduce.93.cloned.1.call-update) | async-done | bytes 262160 | tf_op jit(solution)/shard_map/psum | solution.py:107
  374.9 7.4 fusion.12
  382.4 35.2 %all-reduce.95.cloned.1.call-done = f32[64,1024]{1,0:T(8,128)} async-done(((f32[64,1024]{1,0:T(8,128)}), f32[64,1024]{1,0:T(8,128)}) %all-reduce.95.cloned.1.call-update) | async-done | bytes 262160 | tf_op jit(solution)/shard_map/psum | solution.py:107
  418.6 5.5 collective-permute-start.13
  426.0 3.0 collective-permute-done.12
  430.4 11.1 %psum.188 = f32[]{:T(128)} all-reduce(f32[]{:T(128)} %get-tuple-element.19), channel_id=1, replica_groups=mesh['tm'=2,'gz'=4,'view'=4] {'tm','gz'}, use_global_device_ids=true, to_apply=%region_22.23 | all-reduce | flops 1 | bytes 8 | tf_op jit(solution)/shard_map/psum | solution.py:96
  442.2 4.2 collective-permute-start.15
  448.3 3.0 collective-permute-done.14
  452.6 13.7 %psum.189 = f32[]{:T(128)} all-reduce(f32[]{:T(128)} %get-tuple-element.17), channel_id=1, replica_groups=mesh['tm'=2,'gz'=4,'view'=4] {'tm','gz'}, use_global_device_ids=true, to_apply=%region_24.25 | all-reduce | flops 1 | bytes 8 | tf_op jit(solution)/shard_map/psum | solution.py:96
  467.0 7.4 fusion.32
  474.5 35.5 %all-reduce.97.cloned.1.call-done = f32[64,1024]{1,0:T(8,128)} async-done(((f32[64,1024]{1,0:T(8,128)}), f32[64,1024]{1,0:T(8,128)}) %all-reduce.97.cloned.1.call-update) | async-done | bytes 262160 | tf_op jit(solution)/shard_map/psum | solution.py:107
  511.0 7.4 fusion.8
  518.5 35.2 %all-reduce.99.cloned.1.call-done = f32[64,1024]{1,0:T(8,128)} async-done(((f32[64,1024]{1,0:T(8,128)}), f32[64,1024]{1,0:T(8,128)}) %all-reduce.99.cloned.1.call-update) | async-done | bytes 262160 | tf_op jit(solution)/shard_map/psum | solution.py:107
  554.7 5.5 collective-permute-start.17
  562.2 3.0 collective-permute-done.16
  566.5 11.1 %psum.192 = f32[]{:T(128)} all-reduce(f32[]{:T(128)} %get-tuple-element.15), channel_id=1, replica_groups=mesh['tm'=2,'gz'=4,'view'=4] {'tm','gz'}, use_global_device_ids=true, to_apply=%region_28.29 | all-reduce | flops 1 | bytes 8 | tf_op jit(solution)/shard_map/psum | solution.py:96
  578.3 4.2 collective-permute-start.19
  582.5 2.1 collective-permute-start.18
  584.7 2.8 collective-permute-done.18
  588.8 13.7 %psum.193 = f32[]{:T(128)} all-reduce(f32[]{:T(128)} %get-tuple-element.13), channel_id=1, replica_groups=mesh['tm'=2,'gz'=4,'view'=4] {'tm','gz'}, use_global_device_ids=true, to_apply=%region_30.31 | all-reduce | flops 1 | bytes 8 | tf_op jit(solution)/shard_map/psum | solution.py:96
  603.1 7.4 fusion.28
  610.6 35.5 %all-reduce.101.cloned.1.call-done = f32[64,1024]{1,0:T(8,128)} async-done(((f32[64,1024]{1,0:T(8,128)}), f32[64,1024]{1,0:T(8,128)}) %all-reduce.101.cloned.1.call-update) | async-done | bytes 262160 | tf_op jit(solution)/shard_map/psum | solution.py:107
  647.2 7.4 fusion.4
  654.6 35.2 %all-reduce.103.cloned.1.call-done = f32[64,1024]{1,0:T(8,128)} async-done(((f32[64,1024]{1,0:T(8,128)}), f32[64,1024]{1,0:T(8,128)}) %all-reduce.103.cloned.1.call-update) | async-done | bytes 262160 | tf_op jit(solution)/shard_map/psum | solution.py:107
  690.8 5.5 collective-permute-start.21
  698.3 3.0 collective-permute-done.20
  702.6 11.1 %psum.196 = f32[]{:T(128)} all-reduce(f32[]{:T(128)} %get-tuple-element.11), channel_id=1, replica_groups=mesh['tm'=2,'gz'=4,'view'=4] {'tm','gz'}, use_global_device_ids=true, to_apply=%region_34.35 | all-reduce | flops 1 | bytes 8 | tf_op jit(solution)/shard_map/psum | solution.py:96
  714.4 4.2 collective-permute-start.23
  720.6 3.0 collective-permute-done.22
  724.9 13.7 %psum.197 = f32[]{:T(128)} all-reduce(f32[]{:T(128)} %get-tuple-element.9), channel_id=1, replica_groups=mesh['tm'=2,'gz'=4,'view'=4] {'tm','gz'}, use_global_device_ids=true, to_apply=%region_36.37 | all-reduce | flops 1 | bytes 8 | tf_op jit(solution)/shard_map/psum | solution.py:96
  739.2 7.4 fusion.24
  746.7 35.5 %all-reduce.105.cloned.1.call-done = f32[64,1024]{1,0:T(8,128)} async-done(((f32[64,1024]{1,0:T(8,128)}), f32[64,1024]{1,0:T(8,128)}) %all-reduce.105.cloned.1.call-update) | async-done | bytes 262160 | tf_op jit(solution)/shard_map/psum | solution.py:107
  783.3 7.4 fusion
  790.7 35.2 %all-reduce.107.cloned.1.call-done = f32[64,1024]{1,0:T(8,128)} async-done(((f32[64,1024]{1,0:T(8,128)}), f32[64,1024]{1,0:T(8,128)}) %all-reduce.107.cloned.1.call-update) | async-done | bytes 262160 | tf_op jit(solution)/shard_map/psum | solution.py:107
  (173 shorter events, 46.8 us)
Async XLA Ops:
  6.5 14.2 %copy-start = (f32[64,1024]{1,0:T(8,128)S(1)}, f32[64,1024]{1,0:T(8,128)}, u32[]{:S(2)}) copy-start(f32[64,1024]{1,0:T(8,128)} %param.6) | copy-start | bytes 786436
  6.5 14.1 %copy-start.1 = (bf16[2,2,64,2560]{3,2,1,0:T(8,128)(2,1)S(1)}, bf16[2,2,64,2560]{3,2,1,0:T(8,128)(2,1)}, u32[]{:S(2)}) copy-start(bf16[2,2,64,2560]{3,2,1,0:T(8,128)(2,1)} %param.4) | copy-start | bytes 3932164
  6.5 33.3 %copy-start.2 = (s32[2]{0:T(128)S(1)}, s32[2]{0:T(128)}, u32[]{:S(2)}) copy-start(s32[2]{0:T(128)} %param.7) | copy-start | bytes 28
  6.5 95.1 %all-reduce.85.cloned.1.call-start = ((), (), s32[]{:S(2)}) async-start(), calls=%async_computation | async-start | bytes 524288 | tf_op jit(solution)/shard_map/psum | solution.py:107
  7.4 13.3 %collective-permute-start.1 = (f32[1,1024]{1,0:T(1,128)S(1)}, f32[1,1024]{1,0:T(1,128)S(1)}, u32[]{:S(2)}, u32[]{:S(2)}) collective-permute-start(f32[1,1024]{1,0:T(1,128)S(1)} %get-tuple-element.93), channel_id=1, source_target_pairs={{0,4},{4,8},{8,12},{12,16},{16,20},{20,24},{24,28},{1,5},{5,9},{9,... | collective-permute-start | bytes 12296 | tf_op jit(solution)/shard_map/ppermute | solution.py:24
  11.1 9.6 %collective-permute-start = (f32[1,1024]{1,0:T(1,128)S(1)}, f32[1,1024]{1,0:T(1,128)S(1)}, u32[]{:S(2)}, u32[]{:S(2)}) collective-permute-start(f32[1,1024]{1,0:T(1,128)S(1)} %get-tuple-element.94), channel_id=1, source_target_pairs={{4,0},{8,4},{12,8},{16,12},{20,16},{24,20},{28,24},{5,1},{9,5},{13... | collective-permute-start | bytes 12296 | tf_op jit(solution)/shard_map/ppermute | solution.py:27
  35.1 9.4 %collective-permute-start.3 = (f32[1,1024]{1,0:T(1,128)S(1)}, f32[1,1024]{1,0:T(1,128)S(1)}, u32[]{:S(2)}, u32[]{:S(2)}) collective-permute-start(f32[1,1024]{1,0:T(1,128)S(1)} %get-tuple-element.91), channel_id=1, source_target_pairs={{0,4},{4,8},{8,12},{12,16},{16,20},{20,24},{24,28},{1,5},{5,9},{9,... | collective-permute-start | bytes 12296 | tf_op jit(solution)/shard_map/ppermute | solution.py:24
  37.6 7.0 collective-permute-start.2
  66.4 78.8 %all-reduce.87.cloned.1.call-start = ((), (), s32[]{:S(2)}) async-start(), calls=%async_computation.1 | async-start | bytes 524288 | tf_op jit(solution)/shard_map/psum | solution.py:107
  110.1 127.7 %all-reduce.89.cloned.1.call-start = ((), (), s32[]{:S(2)}) async-start(), calls=%async_computation.2 | async-start | bytes 524288 | tf_op jit(solution)/shard_map/psum | solution.py:107
  146.3 7.5 collective-permute-start.5
  151.8 4.9 collective-permute-start.4
  169.9 6.1 collective-permute-start.7
  174.1 4.9 collective-permute-start.6
  202.1 79.3 %all-reduce.91.cloned.1.call-start = ((), (), s32[]{:S(2)}) async-start(), calls=%async_computation.3 | async-start | bytes 524288 | tf_op jit(solution)/shard_map/psum | solution.py:107
  246.2 127.7 %all-reduce.93.cloned.1.call-start = ((), (), s32[]{:S(2)}) async-start(), calls=%async_computation.4 | async-start | bytes 524288 | tf_op jit(solution)/shard_map/psum | solution.py:107
  282.4 7.5 collective-permute-start.9
  288.0 4.9 collective-permute-start.8
  306.0 6.1 collective-permute-start.11
  310.2 4.9 collective-permute-start.10
  338.3 79.3 %all-reduce.95.cloned.1.call-start = ((), (), s32[]{:S(2)}) async-start(), calls=%async_computation.5 | async-start | bytes 524288 | tf_op jit(solution)/shard_map/psum | solution.py:107
  382.3 127.7 %all-reduce.97.cloned.1.call-start = ((), (), s32[]{:S(2)}) async-start(), calls=%async_computation.6 | async-start | bytes 524288 | tf_op jit(solution)/shard_map/psum | solution.py:107
  418.6 7.5 collective-permute-start.13
  424.1 4.9 collective-permute-start.12
  442.2 6.1 collective-permute-start.15
  446.4 4.9 collective-permute-start.14
  474.4 79.3 %all-reduce.99.cloned.1.call-start = ((), (), s32[]{:S(2)}) async-start(), calls=%async_computation.7 | async-start | bytes 524288 | tf_op jit(solution)/shard_map/psum | solution.py:107
  518.4 127.7 %all-reduce.101.cloned.1.call-start = ((), (), s32[]{:S(2)}) async-start(), calls=%async_computation.8 | async-start | bytes 524288 | tf_op jit(solution)/shard_map/psum | solution.py:107
  554.7 7.5 collective-permute-start.17
  560.2 4.9 collective-permute-start.16
  578.3 6.3 collective-permute-start.19
  582.5 4.9 collective-permute-start.18
  610.5 79.3 %all-reduce.103.cloned.1.call-start = ((), (), s32[]{:S(2)}) async-start(), calls=%async_computation.9 | async-start | bytes 524288 | tf_op jit(solution)/shard_map/psum | solution.py:107
  654.6 127.7 %all-reduce.105.cloned.1.call-start = ((), (), s32[]{:S(2)}) async-start(), calls=%async_computation.10 | async-start | bytes 524288 | tf_op jit(solution)/shard_map/psum | solution.py:107
  690.8 7.5 collective-permute-start.21
  696.3 4.9 collective-permute-start.20
  714.4 6.1 collective-permute-start.23
  718.6 4.9 collective-permute-start.22
  746.6 79.3 %all-reduce.107.cloned.1.call-start = ((), (), s32[]{:S(2)}) async-start(), calls=%async_computation.11 | async-start | bytes 524288 | tf_op jit(solution)/shard_map/psum | solution.py:107
Sparse Core Ops, SparseCore 0:
  66.5 35.0 all-reduce.84
  110.2 35.0 all-reduce.86
  202.3 35.4 all-reduce.88
  246.3 35.0 all-reduce.90
  338.4 35.4 all-reduce.92
  382.5 35.0 all-reduce.94
  474.5 35.4 all-reduce.96
  518.6 35.0 all-reduce.98
  610.6 35.4 all-reduce.100
  654.7 35.0 all-reduce.102
  746.8 35.4 all-reduce.104
  790.8 35.0 all-reduce.106
where the time goes:
time: 841 us; the launch traced here: 835 us
  waiting for transfers between devices  447 us (53%)
  blocking collectives  155 us (18%)
  matrix products  88.6 us (11%)
  starting transfers between devices  79 us (9%)
  other arithmetic  36.1 us (4%)
  between operations  27 us (3%)
    psum x12, waiting for transfers between devices, body(): summed = lax.psum(partial_back, 'view')  417 us
    psum x12, blocking collectives, body(): lax.psum(jnp.sum(gradient * gradient), ('tm', 'gz')) / cell_count  148 us
    dot_general x12, matrix products, project(): lax.dot_general(mismatch, ray_tile, (((1,), (1,)), ((), ())), preferred_e...  88.6 us
    ppermute x12, starting transfers between devices, padded(): lax.ppermute(lax.slice_in_dim(block, block.shape[dim] - width, None, axis...  54.7 us
    ppermute x12, waiting for transfers between devices, padded(): lax.ppermute(lax.slice_in_dim(block, 0, width, axis=dim), axis, backward)  29.7 us
    ppermute x12, starting transfers between devices, padded(): lax.ppermute(lax.slice_in_dim(block, 0, width, axis=dim), axis, backward)  23.6 us
  transfers between devices with their start and end apart: 36, of which 22 were waited for; matrix products, arithmetic and copies ran while one was open for 1% of the time, Pallas kernels for 0%

commit v1 on v0

v1 whole, which is shorter than its diff:
```python
import functools

import jax
import jax.numpy as jnp
from jax import lax
from jax.experimental import pallas as pl
from jax.experimental.pallas import tpu as pltpu
from jax.sharding import PartitionSpec as P

RY = 128
FRAMES = 2
SWEEPS = 3
TV_STEPS = 2
RELAXATION = 0.9
STEP_SCALE = 0.3
STEP_DECAY = 0.7
SMOOTHING = 0.01
NORM_GUARD = 1e-06
RIM = 8

MESH = pl.DeviceIdType.MESH


def slab_device(index, gz):
    return {"tm": lax.div(index, gz), "gz": lax.rem(index, gz)}


def iterate_kernel(
    slabs, gz, gram_ref, back_ref, cover_ref, warm_ref, out_ref,
    xs, grad, fluxz, defect, own, stat, rim, stat_send, stat_recv, rim_send, rim_recv,
):
    me = lax.axis_index("tm") * gz + lax.axis_index("gz")
    ext, pixels = warm_ref.shape
    rows = ext - 2 * RIM
    depth_total = slabs * rows
    per_view = gram_ref.shape[0]
    tiles = pixels // RY

    barrier = pltpu.get_barrier_semaphore()
    for d in range(1, slabs):
        pl.semaphore_signal(
            barrier, inc=1, device_id=slab_device(lax.rem(me + d, slabs), gz), device_id_type=MESH
        )

    xs[:ext] = warm_ref[...]
    xs[ext:] = jnp.zeros((8, pixels), jnp.float32)
    fluxz[:8] = jnp.zeros((8, pixels), jnp.float32)
    ones = jnp.ones((16, pixels), jnp.bfloat16)
    for slot in range(per_view):
        row_sum = jnp.dot(ones, gram_ref[slot], preferred_element_type=jnp.float32)
        defect[slot] = cover_ref[slot : slot + 1] - row_sum[:8]
    zrow = lax.broadcasted_iota(jnp.int32, (ext, RY), 0) + (me * rows - RIM)
    column = lax.broadcasted_iota(jnp.int32, (ext, RY), 1)

    pl.semaphore_wait(barrier, slabs - 1)

    def tv_step(step, scale):
        zmask = ((zrow >= 0) & (zrow < depth_total - 1)).astype(jnp.float32)
        cmask = (column < RY - 1).astype(jnp.float32)
        total = jnp.zeros((8, RY), jnp.float32)
        before = None
        here = xs[:ext, :RY]
        for i in range(tiles):
            lanes = slice(i * RY, (i + 1) * RY)
            dz = (xs[1 : ext + 1, lanes] - here) * zmask
            dc = (pltpu.roll(here, RY - 1, 1) - here) * cmask
            square = dz * dz + dc * dc + SMOOTHING
            if i < tiles - 1:
                after = xs[:ext, (i + 1) * RY : (i + 2) * RY]
                di = after - here
                square = square + di * di
            inverse = lax.rsqrt(square)
            fz = dz * inverse
            fc = dc * inverse
            fluxz[8:, lanes] = fz
            g = (fluxz[7 : ext + 7, lanes] - fz) + (pltpu.roll(fc, 1, 1) - fc)
            if before is not None:
                g = g + before
            if i < tiles - 1:
                fi = di * inverse
                g = g - fi
                before = fi
                here = after
            grad[:, lanes] = g
            mine = g[RIM : RIM + rows]
            total = total + jnp.sum((mine * mine).reshape(rows // 8, 8, RY), axis=0)
        own[step] = total
        sends = []
        for d in range(1, slabs):
            copy = pltpu.make_async_remote_copy(
                src_ref=own.at[step],
                dst_ref=stat.at[step, me],
                send_sem=stat_send.at[step, d],
                recv_sem=stat_recv.at[step, d],
                device_id=slab_device(lax.rem(me + d, slabs), gz),
                device_id_type=MESH,
            )
            copy.start()
            sends.append(copy)
        for d in range(1, slabs):
            source = lax.rem(me + slabs - d, slabs)
            pltpu.make_async_remote_copy(
                src_ref=own.at[step],
                dst_ref=stat.at[step, source],
                send_sem=stat_send.at[step, d],
                recv_sem=stat_recv.at[step, d],
                device_id=slab_device(source, gz),
                device_id_type=MESH,
            ).wait_recv()
        for d in range(1, slabs):
            source = lax.rem(me + slabs - d, slabs)
            total = total + stat[step, source]
        for copy in sends:
            copy.wait_send()
        mean = jnp.sum(total, keepdims=True) / (depth_total * pixels)
        factor = scale * lax.rsqrt(mean + NORM_GUARD)
        xs[:ext] = xs[:ext] - factor * grad[...]

    def sart(frame, n):
        x = xs[:ext]
        xb = x.astype(jnp.bfloat16)
        centre = jnp.sum(x, axis=1, keepdims=True) * (1.0 / pixels)
        width = 256
        for lo in range(0, pixels, width):
            lanes = slice(lo, lo + width)
            y = jnp.dot(xb, gram_ref[n, :, lanes], preferred_element_type=jnp.float32)
            y = y + centre * defect[n, 0:1, lanes]
            change = (back_ref[frame, n, :, lanes] - y) * (RELAXATION / cover_ref[n : n + 1, lanes])
            xs[:ext, lanes] = jnp.maximum(x[:, lanes] + change, 0.0)

    up, down = lax.rem(me + 1, slabs), lax.rem(me + slabs - 1, slabs)

    for frame in range(FRAMES):
        if frame > 0:
            copies = []
            for side, (source, target) in enumerate(((rows, up), (RIM, down))):
                copy = pltpu.make_async_remote_copy(
                    src_ref=xs.at[pl.ds(source, RIM)],
                    dst_ref=rim.at[frame - 1, side],
                    send_sem=rim_send.at[frame - 1, side],
                    recv_sem=rim_recv.at[frame - 1, side],
                    device_id=slab_device(target, gz),
                    device_id_type=MESH,
                )
                copy.start()
                copies.append(copy)
            for copy in copies:
                copy.wait()
            xs[:RIM] = rim[frame - 1, 0]
            xs[RIM + rows : ext] = rim[frame - 1, 1]

        def sweep_body(sweep, carry, frame=frame):
            for k in range(TV_STEPS):
                scale = jnp.float32(0.0)
                for s in range(SWEEPS):
                    value = STEP_SCALE * STEP_DECAY ** (s * TV_STEPS + k)
                    scale = jnp.where(sweep == s, jnp.float32(value), scale)
                tv_step((frame * SWEEPS + sweep) * TV_STEPS + k, scale)
            for n in range(per_view):
                sart(frame, n)
            return carry

        lax.fori_loop(0, SWEEPS, sweep_body, 0)
        out_ref[frame] = xs[RIM : RIM + rows]


def iterate(gram, back, cover, warm, slabs, gz):
    ext, pixels = warm.shape
    rows = ext - 2 * RIM
    steps = FRAMES * SWEEPS * TV_STEPS
    vmem = pl.BlockSpec(memory_space=pltpu.VMEM)
    return pl.pallas_call(
        functools.partial(iterate_kernel, slabs, gz),
        out_shape=jax.ShapeDtypeStruct((FRAMES, rows, pixels), jnp.float32),
        in_specs=[vmem] * 4,
        out_specs=vmem,
        scratch_shapes=[
            pltpu.VMEM((ext + 8, pixels), jnp.float32),
            pltpu.VMEM((ext, pixels), jnp.float32),
            pltpu.VMEM((ext + 8, pixels), jnp.float32),
            pltpu.VMEM((gram.shape[0], 8, pixels), jnp.float32),
            pltpu.VMEM((steps, 8, RY), jnp.float32),
            pltpu.VMEM((steps, slabs, 8, RY), jnp.float32),
            pltpu.VMEM((FRAMES - 1, 2, RIM, pixels), jnp.float32),
            pltpu.SemaphoreType.DMA((steps, slabs)),
            pltpu.SemaphoreType.DMA((steps, slabs)),
            pltpu.SemaphoreType.DMA((FRAMES - 1, 2)),
            pltpu.SemaphoreType.DMA((FRAMES - 1, 2)),
        ],
        compiler_params=pltpu.CompilerParams(
            collective_id=0, has_side_effects=True, vmem_limit_bytes=40 * 2**20
        ),
    )(gram, back, cover, warm)


def with_rims(block, dim, count):
    forward = [(i, (i + 1) % count) for i in range(count)]
    backward = [(target, source) for source, target in forward]
    axes = ("tm", "gz")
    low = lax.ppermute(
        lax.slice_in_dim(block, block.shape[dim] - RIM, None, axis=dim), axes, forward
    )
    high = lax.ppermute(lax.slice_in_dim(block, 0, RIM, axis=dim), axes, backward)
    return jnp.concatenate([low, block, high], axis=dim)


def body(tm, gz, sinogram, projector, warm_volume, view_order):
    slices, pixels = warm_volume.shape
    per_view = projector.shape[0]
    slabs = tm * gz
    slab = lax.axis_index("tm") * gz + lax.axis_index("gz")
    share = pixels // slabs
    ray_sums = jnp.sum(projector, axis=1, dtype=jnp.float32)
    cover = lax.psum(jnp.sum(projector, axis=2, dtype=jnp.float32), "view")
    rays = 1.0 / ray_sums[:, None, :]
    part = lax.dynamic_slice_in_dim(projector, slab * share, share, axis=1)
    weighted = (part.astype(jnp.float32) * rays).astype(jnp.bfloat16)
    measured = (sinogram.astype(jnp.float32) * rays[None]).astype(jnp.bfloat16)
    measured = jnp.swapaxes(measured, 0, 1).reshape(per_view, FRAMES * slices, -1)
    left = jnp.concatenate([weighted, measured], axis=1)
    product = jnp.einsum("jmd,jpd->jmp", left, projector, preferred_element_type=jnp.float32)
    gram = lax.psum_scatter(product[:, :share], "view", scatter_dimension=1, tiled=True)
    gram = lax.all_gather(
        gram.astype(jnp.bfloat16), ("tm", "gz", "view"), axis=1, tiled=True
    )
    back = lax.psum(product[:, share:], "view").reshape(per_view, FRAMES, slices, pixels)
    back = jnp.swapaxes(back, 0, 1)
    gram = jnp.take(gram, view_order, axis=0)
    back = jnp.take(back, view_order, axis=1)
    cover = jnp.take(cover, view_order, axis=0)
    return iterate(
        gram, with_rims(back, 2, slabs), cover, with_rims(warm_volume, 0, slabs), slabs, gz
    )


def solution(mesh):
    return jax.shard_map(
        functools.partial(body, mesh.shape["tm"], mesh.shape["gz"]),
        mesh=mesh,
        in_specs=(
            P(None, "view", ("tm", "gz"), None),
            P("view", None, None),
            P(("tm", "gz"), None),
            P(),
        ),
        out_specs=P(None, ("tm", "gz"), None),
        check_vma=False,
    )
```

time: 841 us -> 250 us (0.30)
  waiting for transfers between devices: 447 us -> 127 us
  blocking collectives: 155 us -> 8.28 us
  matrix products: 88.6 us -> 5.63 us
  starting transfers between devices: 79 us -> 4.09 us
  Pallas kernels: 0 us -> 57.1 us
  other arithmetic: 36.1 us -> 14.3 us
  local copies, waits for them, and re-layouts: 2 us -> 17.4 us
  between operations: 27 us -> 13.3 us
    psum x12 -> x1, waiting for transfers between devices: 417 us -> 41.3 us  [body(): lax.psum(product[:, share:], 'view')]
    psum x13 -> x1, blocking collectives: 155 us -> 8.28 us  [body(): cover = lax.psum(jnp.sum(projector, axis=2, dtype=jnp.float32), 'view')]
    dot_general x12 -> x1, matrix products: 88.6 us -> 5.63 us  [body(): jnp.einsum('jmd,jpd->jmp', left, projector, preferred_element_type=jnp.fl...]
    ppermute x24 -> x4, starting transfers between devices: 78.3 us -> 4.01 us  [the longest x2 2.5 us: with_rims(): lax.ppermute(lax.slice_in_dim(block, block.shape[dim] - RIM, None, axis=d...]
    all_gather x0 -> x1, waiting for transfers between devices: none -> 57.4 us  [body(): lax.all_gather(gram.astype(jnp.bfloat16), ('tm', 'gz', 'view'), axis=1, t...]
    pallas_call x0 -> x1, Pallas kernels: none -> 57.1 us  [iterate(): pl.pallas_call(functools.partial(iterate_kernel, slabs, gz), out_shape=ja...]
    ppermute x24 -> x4, waiting for transfers between devices: 29.7 us -> 3.21 us  [the longest x2 2.29 us: with_rims(): lax.ppermute(lax.slice_in_dim(block, 0, RIM, axis=dim), axes, backward)]
    reduce_scatter x0 -> x1, waiting for transfers between devices: none -> 24.8 us  [body(): lax.psum_scatter(product[:, :share], 'view', scatter_dimension=1, tiled=T...]
  transfers between devices with their start and end apart: 36 -> 7, of which waited for: 22 -> 5; matrix products, arithmetic and copies ran while one was open for 1% -> 2% of each run, Pallas kernels for 0% -> 0%
where the time goes in v1:
time: 250 us; the launch traced here: 247 us
  waiting for transfers between devices  127 us (51%)
  Pallas kernels  57.1 us (23%)
  local copies, waits for them, and re-layouts  17.4 us (7%)
  other arithmetic  14.3 us (6%)
  between operations  13.3 us (5%)
  blocking collectives  8.28 us (3%)
  matrix products  5.63 us (2%)
  starting transfers between devices  4.09 us (2%)
    all_gather x1, waiting for transfers between devices, body(): lax.all_gather(gram.astype(jnp.bfloat16), ('tm', 'gz', 'view'), axis=1, t...  57.4 us
    pallas_call x1, Pallas kernels, iterate(): pl.pallas_call(functools.partial(iterate_kernel, slabs, gz), out_shape=ja...  57.1 us
    psum x1, waiting for transfers between devices, body(): lax.psum(product[:, share:], 'view')  41.3 us
    reduce_scatter x1, waiting for transfers between devices, body(): lax.psum_scatter(product[:, :share], 'view', scatter_dimension=1, tiled=T...  24.8 us
    gather x3, local copies, waits for them, and re-layouts, body(): gram = jnp.take(gram, view_order, axis=0)  11.8 us
    psum x1, blocking collectives, body(): cover = lax.psum(jnp.sum(projector, axis=2, dtype=jnp.float32), 'view')  8.28 us
    reduce_sum x1, other arithmetic, body(): cover = lax.psum(jnp.sum(projector, axis=2, dtype=jnp.float32), 'view')  7.57 us
    dot_general x1, matrix products, body(): jnp.einsum('jmd,jpd->jmp', left, projector, preferred_element_type=jnp.fl...  5.63 us
  transfers between devices with their start and end apart: 7, of which 5 were waited for; matrix products, arithmetic and copies ran while one was open for 2% of the time, Pallas kernels for 0%

profile of v1, /device:TPU:25, one launch (start us, length us, event | category | flops | bytes accessed | tf_op | source)
XLA Modules:
  0.0 246.9 jit_solution(341736902942564904)
XLA Ops:
  6.5 0.0 reduce-scatter.2.cloned.1.call-start
  6.5 0.0 copy-start
  6.5 7.6 %convert_reduce_fusion = (f32[2,1024]{1,0:T(2,128)S(1)}, f32[2,2560]{1,0:T(2,128)S(1)}) fusion(bf16[2,1024,2560]{2,1,0:T(8,128)(2,1)} %param.5), kind=kLoop, calls=%fused_computation.4 | loop fusion | flops 15721472 | bytes 10514432 | tf_op jit(solution)/shard_map/reduce_sum | solution.py:214
  14.1 0.0 copy-done
  14.1 0.2 fusion.4
  14.4 0.1 copy.6
  14.5 1.5 multiply_convert_fusion.1
  16.0 5.6 %fusion = f32[2,256,1024]{2,1,0:T(8,128)S(1)} fusion(bf16[2,1024,2560]{2,1,0:T(8,128)(2,1)} %param.5, bf16[2,128,2560]{2,1,0:T(8,128)(2,1)S(1)} %bitcast.12, bf16[2,128,2560]{2,1,0:T(8,128)(2,1)S(1)} %multiply_convert_fusion.1), kind=kOutput, calls=%fused_computation.7 | convolution fusion | flops 2689597440 | bytes 15204352 | tf_op jit(solution)/shard_map/jmd,jpd->jmp/dot_general | solution.py:221
  21.7 1.2 fusion.8
  22.8 0.0 reduce-scatter.2.cloned.1.call-update
  22.9 0.0 copy-start.1
  22.9 0.0 copy-start.2
  22.9 0.0 all-reduce.2.cloned.1.call-start
  22.9 1.1 copy.13
  24.0 0.0 all-reduce.2.cloned.1.call-update
  24.0 0.0 all-gather.2.cloned.1.call-start
  24.1 24.8 %reduce-scatter.2.cloned.1.call-done = f32[2,32,1024]{2,1,0:T(8,128)} async-done(((f32[2,128,1024]{2,1,0:T(8,128)}), f32[2,32,1024]{2,1,0:T(8,128)}) %reduce-scatter.2.cloned.1.call-update) | async-done | bytes 262160 | tf_op jit(solution)/shard_map/reduce_scatter | solution.py:222
  48.9 1.6 convert_element_type.24
  50.5 0.0 all-gather.2.cloned.1.call-update
  50.5 0.0 copy-done.1
  50.6 0.7 collective-permute-start.3
  51.2 1.2 collective-permute-start.2
  52.4 8.3 %psum.15 = f32[2,1024]{1,0:T(2,128)S(1)} all-reduce(f32[2,1024]{1,0:T(2,128)S(1)} %get-tuple-element.5), channel_id=1, replica_groups=mesh['tm'=2,'gz'=4,'view'=4] {'view'}, use_global_device_ids=true, to_apply=%region_4.0 | all-reduce | flops 2048 | bytes 16384 | tf_op jit(solution)/shard_map/psum | solution.py:214
  60.7 0.0 copy-done.2
  60.8 0.6 gather_fusion.1
  61.3 41.3 %all-reduce.2.cloned.1.call-done = f32[2,2,64,1024]{3,2,1,0:T(8,128)} async-done(((f32[2,2,64,1024]{3,2,1,0:T(8,128)}), f32[2,2,64,1024]{3,2,1,0:T(8,128)}) %all-reduce.2.cloned.1.call-update) | async-done | bytes 1048592 | tf_op jit(solution)/shard_map/psum | solution.py:226
  102.7 1.8 gather_fusion
  104.5 0.2 fusion.5
  104.7 0.8 collective-permute-start.1
  105.6 1.3 collective-permute-start
  106.9 0.1 broadcast_select_fusion.cover_ref
  107.0 0.0 collective-permute-done.3
  107.0 0.0 collective-permute-done.2
  107.0 2.3 collective-permute-done.1
  109.3 0.9 collective-permute-done
  110.2 0.1 pad_maximum_fusion.back_ref
  110.3 57.4 %all-gather.2.cloned.1.call-done = bf16[2,1024,1024]{2,1,0:T(8,128)(2,1)} async-done(((bf16[2,32,1024]{2,1,0:T(8,128)(2,1)}), bf16[2,1024,1024]{2,1,0:T(8,128)(2,1)}) %all-gather.2.cloned.1.call-update) | async-done | bytes 4194320 | tf_op jit(solution)/shard_map/all_gather | solution.py:223
  167.7 4.6 %fusion.7 = (bf16[2,512,1024]{2,1,0:T(8,128)(2,1)}, bf16[2,512,1024]{2,1,0:T(8,128)(2,1)}) fusion(bf16[2,1024,1024]{2,1,0:T(8,128)(2,1)} %all-gather.2.cloned.1.call-done), kind=kLoop, calls=%fused_computation.25 | loop fusion | bytes 8388608 | tf_op jit(solution)/shard_map/jit(_take)/gather | solution.py:228
  172.3 3.6 %gather_fusion.3 = bf16[2,512,1024]{2,1,0:T(8,128)(2,1)} fusion(bf16[2,512,1024]{2,1,0:T(8,128)(2,1)} %get-tuple-element.8, s32[1024]{0:T(1024)S(1)} %pad_clamp_fusion), kind=kCustom, calls=%fused_computation.3 | custom fusion | bytes 4194312 | tf_op jit(solution)/shard_map/jit(_take)/gather | solution.py:228
  175.9 3.6 %gather_fusion.2 = bf16[2,512,1024]{2,1,0:T(8,128)(2,1)} fusion(bf16[2,512,1024]{2,1,0:T(8,128)(2,1)} %get-tuple-element.7, s32[1024]{0:T(1024)S(1)} %pad_clamp_fusion), kind=kCustom, calls=%fused_computation.2 | custom fusion | bytes 4194312 | tf_op jit(solution)/shard_map/jit(_take)/gather | solution.py:228
  179.5 3.0 %maximum_select_fusion.gram_ref = bf16[2,1024,1024]{2,1,0:T(8,128)(2,1)S(1)} fusion(bf16[2,512,1024]{2,1,0:T(8,128)(2,1)} %gather_fusion.3, bf16[2,512,1024]{2,1,0:T(8,128)(2,1)} %gather_fusion.2, pred[2]{0:T(512)(128)(4,1)S(1)} %compare_and_fusion), kind=kLoop, calls=%fused_computation.6 | loop fusion | flops 10485760 | bytes 8388610 | tf_op jit(solution)/shard_map/jit(_take)/select_n | solution.py:228
  182.5 57.1 %shard_map.46 = f32[2,64,1024]{2,1,0:T(8,128)S(1)} custom-call(bf16[2,1024,1024]{2,1,0:T(8,128)(2,1)S(1)} %maximum_select_fusion.gram_ref, f32[2,2,80,1024]{3,2,1,0:T(8,128)S(1)} %pad_maximum_fusion.back_ref, f32[2,1024]{1,0:T(2,128)S(1)} %broadcast_select_fusion.cover_ref, f32[80,1024]{1,0:T(8,128)S(1)} %pad_maximum_fusion.1.warm_ref), custom_call_target="tpu_custom_call" | custom-call | tf_op jit(solution)/shard_map/pallas_call | solution.py:172
  239.6 0.8 copy.16
  (7 shorter events, 0.1 us)
Async XLA Ops:
  6.5 42.4 %reduce-scatter.2.cloned.1.call-start = ((), (), s32[]{:S(2)}) async-start(), calls=%async_computation.1 | async-start | bytes 1310720 | tf_op jit(solution)/shard_map/reduce_scatter | solution.py:222
  6.5 7.6 %copy-start = (bf16[2,2,64,2560]{3,2,1,0:T(8,128)(2,1)S(1)}, bf16[2,2,64,2560]{3,2,1,0:T(8,128)(2,1)}, u32[]{:S(2)}) copy-start(bf16[2,2,64,2560]{3,2,1,0:T(8,128)(2,1)} %param.4) | copy-start | bytes 3932164
  22.9 27.7 %copy-start.1 = (f32[64,1024]{1,0:T(8,128)S(1)}, f32[64,1024]{1,0:T(8,128)}, u32[]{:S(2)}) copy-start(f32[64,1024]{1,0:T(8,128)} %param.6) | copy-start | bytes 786436
  22.9 37.8 %copy-start.2 = (s32[2]{0:T(128)S(1)}, s32[2]{0:T(128)}, u32[]{:S(2)}) copy-start(s32[2]{0:T(128)} %param.7) | copy-start | bytes 28
  22.9 79.8 %all-reduce.2.cloned.1.call-start = ((), (), s32[]{:S(2)}) async-start(), calls=%async_computation.3 | async-start | bytes 2097152 | tf_op jit(solution)/shard_map/psum | solution.py:226
  24.0 143.6 %all-gather.2.cloned.1.call-start = ((), (), s32[]{:S(2)}) async-start(), calls=%async_computation.2 | async-start | bytes 4325376 | tf_op jit(solution)/shard_map/all_gather | solution.py:223
  50.6 56.4 %collective-permute-start.3 = (f32[8,1024]{1,0:T(8,128)S(1)}, f32[8,1024]{1,0:T(8,128)S(1)}, u32[]{:S(2)}, u32[]{:S(2)}) collective-permute-start(f32[8,1024]{1,0:T(8,128)S(1)} %get-tuple-element.14), channel_id=1, source_target_pairs={{4,0},{8,4},{12,8},{16,12},{20,16},{24,20},{28,24},{0,28},{5,1},{9... | collective-permute-start | bytes 98312 | tf_op jit(solution)/shard_map/ppermute | solution.py:203
  51.2 55.7 %collective-permute-start.2 = (f32[8,1024]{1,0:T(8,128)S(1)}, f32[8,1024]{1,0:T(8,128)S(1)}, u32[]{:S(2)}, u32[]{:S(2)}) collective-permute-start(f32[8,1024]{1,0:T(8,128)S(1)} %get-tuple-element.13), channel_id=1, source_target_pairs={{0,4},{4,8},{8,12},{12,16},{16,20},{20,24},{24,28},{28,0},{1,5},{5... | collective-permute-start | bytes 98312 | tf_op jit(solution)/shard_map/ppermute | solution.py:200
  104.7 4.6 %collective-permute-start.1 = (f32[2,2,8,1024]{3,2,1,0:T(8,128)S(1)}, f32[2,2,8,1024]{3,2,1,0:T(8,128)S(1)}, u32[]{:S(2)}, u32[]{:S(2)}) collective-permute-start(f32[2,2,8,1024]{3,2,1,0:T(8,128)S(1)} %get-tuple-element.12), channel_id=1, source_target_pairs={{4,0},{8,4},{12,8},{16,12},{20,16},{24,20},{28,24},{0,28},{5,1},{9... | collective-permute-start | bytes 393224 | tf_op jit(solution)/shard_map/ppermute | solution.py:203
  105.6 4.6 %collective-permute-start = (f32[2,2,8,1024]{3,2,1,0:T(8,128)S(1)}, f32[2,2,8,1024]{3,2,1,0:T(8,128)S(1)}, u32[]{:S(2)}, u32[]{:S(2)}) collective-permute-start(f32[2,2,8,1024]{3,2,1,0:T(8,128)S(1)} %get-tuple-element.11), channel_id=1, source_target_pairs={{0,4},{4,8},{8,12},{12,16},{16,20},{20,24},{24,28},{28,0},{1,5},{5... | collective-permute-start | bytes 393224 | tf_op jit(solution)/shard_map/ppermute | solution.py:200
Sparse Core Ops, SparseCore 0:
  23.0 25.8 reduce-scatter.1
  51.4 51.2 all-reduce.1
  105.7 61.9 all-gather.1

commit v2 on v1

v2 whole, which is shorter than its diff:
```python
import functools

import jax
import jax.numpy as jnp
from jax import lax
from jax.experimental import pallas as pl
from jax.experimental.pallas import tpu as pltpu
from jax.sharding import PartitionSpec as P

RY = 128
FRAMES = 2
SWEEPS = 3
TV_STEPS = 2
RELAXATION = 0.9
STEP_SCALE = 0.3
STEP_DECAY = 0.7
SMOOTHING = 0.01
NORM_GUARD = 1e-06
RIM = 8

MESH = pl.DeviceIdType.MESH


def slab_device(index, gz):
    return {"tm": lax.div(index, gz), "gz": lax.rem(index, gz)}


def wrap(index, count):
    return lax.rem(index + count, count)


def remote(src, dst, send, recv, device):
    return pltpu.make_async_remote_copy(
        src_ref=src, dst_ref=dst, send_sem=send, recv_sem=recv,
        device_id=device, device_id_type=MESH,
    )


def iterate_kernel(
    slabs, gz, views, gram_part, back_part, cover_part, warm_ref, out_ref,
    gram, gram_in, back, back_in, cover_in, cover, xs, grad, fluxz, defect, own, stat, rim,
    cover_send, cover_recv, sum_send, sum_recv, view_send, view_recv, layer_send, layer_recv,
    pair_send, pair_recv, part_send, part_recv, full_send, full_recv, edge_send, edge_recv,
    stat_send, stat_recv, rim_send, rim_recv,
):
    me = lax.axis_index("tm") * gz + lax.axis_index("gz")
    mine = lax.axis_index("view")
    rows, pixels = warm_ref.shape
    ext = rows + 2 * RIM
    depth_total = slabs * rows
    per_view = gram.shape[0] // pixels
    tiles = pixels // RY
    share = pixels // slabs
    piece = per_view * share // views
    per_slot = views // per_view
    band = rows // views
    half = slabs // 2
    pair = lax.div(me, 2)
    side = lax.rem(me, 2)
    sibling = me + 1 - 2 * side
    up, down = wrap(me + 1, slabs), wrap(me - 1, slabs)

    def gram_rows(slab, view):
        start = lax.div(view, per_slot) * pixels + slab * share + lax.rem(view, per_slot) * piece
        return pl.ds(pl.multiple_of(start, 16), piece)

    def part_rows(view):
        return pl.ds(pl.multiple_of(view * piece, 16), piece)

    def band_rows(view, base):
        return pl.ds(pl.multiple_of(view * band + base, 8), band)

    def rim_copies(at):
        return [
            remote(
                xs.at[pl.ds(source, RIM)], rim.at[at, s],
                rim_send.at[at, s], rim_recv.at[at, s], slab_device(target, gz),
            )
            for s, (source, target) in enumerate(((rows, up), (RIM, down)))
        ]

    def take_rims(at):
        for copy in rim_copies(at):
            copy.wait()
        xs[:RIM] = rim[at, 0]
        xs[RIM + rows : ext] = rim[at, 1]

    def cover_copy(d, to):
        return remote(
            cover_part, cover_in.at[d], cover_send.at[d], cover_recv.at[d],
            {"view": wrap(mine + to, views)},
        )

    def sum_copy(d):
        target = wrap(mine + d, views)
        return remote(
            gram_part.at[part_rows(target)], gram_in.at[d],
            sum_send.at[d], sum_recv.at[d], {"view": target},
        )

    def view_copy(d, view, target):
        at = gram_rows(me, view)
        return remote(
            gram.at[at], gram.at[at], view_send.at[d], view_recv.at[d], {"view": target}
        )

    def layer_copy(d, e, slab, target):
        at = gram_rows(slab, wrap(mine - d, views))
        return remote(
            gram.at[at], gram.at[at], layer_send.at[d, e], layer_recv.at[d, e],
            slab_device(target, gz),
        )

    def mate(e):
        return wrap(pair + e, half) * 2 + side

    def pair_copy(d, e, slab):
        at = gram_rows(slab, wrap(mine - d, views))
        return remote(
            gram.at[at], gram.at[at], pair_send.at[d, e], pair_recv.at[d, e],
            slab_device(sibling, gz),
        )

    def part_copy(t, d):
        target = wrap(mine + d, views)
        return remote(
            back_part.at[t, :, band_rows(target, 0)], back_in.at[t, d],
            part_send.at[t, d], part_recv.at[t, d], {"view": target},
        )

    def full_copy(t, d, view, target):
        at = back.at[t, :, band_rows(view, RIM)]
        return remote(at, at, full_send.at[t, d], full_recv.at[t, d], {"view": target})

    def edge_copies(t):
        return [
            remote(
                back.at[t, :, pl.ds(source, RIM)], back.at[t, :, pl.ds(dest, RIM)],
                edge_send.at[t, s], edge_recv.at[t, s], slab_device(target, gz),
            )
            for s, (source, dest, target) in enumerate(
                ((rows, 0, up), (RIM, rows + RIM, down))
            )
        ]

    def sum_back(t):
        total = back_part[t, :, band_rows(mine, 0)]
        for d in range(1, views):
            part_copy(t, d).wait_recv()
            total = total + back_in[t, d]
        back[t, :, band_rows(mine, RIM)] = total
        for d in range(1, views):
            full_copy(t, d, mine, wrap(mine + d, views)).start()

    def spread_edges(t):
        for d in range(1, views):
            full_copy(t, d, wrap(mine - d, views), wrap(mine - d, views)).wait_recv()
        for copy in edge_copies(t):
            copy.start()

    def sum_gram():
        total = gram_part[part_rows(mine)].astype(jnp.float32)
        for d in range(1, views):
            sum_copy(d).wait_recv()
            total = total + gram_in[d].astype(jnp.float32)
        gram[gram_rows(me, mine)] = total.astype(jnp.bfloat16)
        for d in range(1, views):
            view_copy(d, mine, wrap(mine + d, views)).start()
        for e in range(1, half):
            layer_copy(0, e, me, mate(e)).start()
        pair_copy(0, 0, me).start()

    def gather_gram():
        for d in range(1, views):
            view_copy(d, wrap(mine - d, views), wrap(mine - d, views)).wait_recv()
            for e in range(1, half):
                layer_copy(d, e, me, mate(e)).start()
            pair_copy(d, 0, me).start()
        for d in range(views):
            for e in range(1, half):
                layer_copy(d, e, mate(-e), mate(-e)).wait_recv()
                pair_copy(d, e, mate(-e)).start()
        for d in range(views):
            for e in range(half):
                pair_copy(d, e, mate(-e) + 1 - 2 * side).wait_recv()

    def weigh():
        for d in range(1, views):
            cover_copy(d, d).wait_recv()
        total = cover_part[...]
        for d in range(1, views):
            total = total + cover_in[d]
        cover[...] = RELAXATION / total
        ones = jnp.ones((16, pixels), jnp.bfloat16)
        for slot in range(per_view):
            row_sum = jnp.dot(
                ones, gram[slot * pixels : (slot + 1) * pixels],
                preferred_element_type=jnp.float32,
            )
            defect[slot] = total[slot : slot + 1] - row_sum[:8]

    barrier = pltpu.get_barrier_semaphore()
    for d in range(1, slabs):
        pl.semaphore_signal(
            barrier, inc=1, device_id=slab_device(wrap(me + d, slabs), gz), device_id_type=MESH
        )
    for d in range(1, views):
        pl.semaphore_signal(
            barrier, inc=1, device_id={"view": wrap(mine + d, views)}, device_id_type=MESH
        )

    xs[RIM : RIM + rows] = warm_ref[...]
    xs[ext:] = jnp.zeros((8, pixels), jnp.float32)
    fluxz[:8] = jnp.zeros((8, pixels), jnp.float32)
    zrow = lax.broadcasted_iota(jnp.int32, (ext, RY), 0) + (me * rows - RIM)
    column = lax.broadcasted_iota(jnp.int32, (ext, RY), 1)

    pl.semaphore_wait(barrier, slabs + views - 2)
    for copy in rim_copies(0):
        copy.start()
    for d in range(1, views):
        sum_copy(d).start()
    for d in range(1, views):
        cover_copy(d, d).start()
    for d in range(1, views):
        part_copy(0, d).start()
    take_rims(0)

    def tv_step(step, scale):
        zmask = ((zrow >= 0) & (zrow < depth_total - 1)).astype(jnp.float32)
        cmask = (column < RY - 1).astype(jnp.float32)
        total = jnp.zeros((8, RY), jnp.float32)
        before = None
        here = xs[:ext, :RY]
        for i in range(tiles):
            lanes = slice(i * RY, (i + 1) * RY)
            dz = (xs[1 : ext + 1, lanes] - here) * zmask
            dc = (pltpu.roll(here, RY - 1, 1) - here) * cmask
            square = dz * dz + dc * dc + SMOOTHING
            if i < tiles - 1:
                after = xs[:ext, (i + 1) * RY : (i + 2) * RY]
                di = after - here
                square = square + di * di
            inverse = lax.rsqrt(square)
            fz = dz * inverse
            fc = dc * inverse
            fluxz[8:, lanes] = fz
            g = (fluxz[7 : ext + 7, lanes] - fz) + (pltpu.roll(fc, 1, 1) - fc)
            if before is not None:
                g = g + before
            if i < tiles - 1:
                fi = di * inverse
                g = g - fi
                before = fi
                here = after
            grad[:, lanes] = g
            inner = g[RIM : RIM + rows]
            total = total + jnp.sum((inner * inner).reshape(rows // 8, 8, RY), axis=0)
        own[step] = total
        sends = []
        for d in range(1, slabs):
            copy = pltpu.make_async_remote_copy(
                src_ref=own.at[step],
                dst_ref=stat.at[step, me],
                send_sem=stat_send.at[step, d],
                recv_sem=stat_recv.at[step, d],
                device_id=slab_device(lax.rem(me + d, slabs), gz),
                device_id_type=MESH,
            )
            copy.start()
            sends.append(copy)
        for d in range(1, slabs):
            source = lax.rem(me + slabs - d, slabs)
            pltpu.make_async_remote_copy(
                src_ref=own.at[step],
                dst_ref=stat.at[step, source],
                send_sem=stat_send.at[step, d],
                recv_sem=stat_recv.at[step, d],
                device_id=slab_device(source, gz),
                device_id_type=MESH,
            ).wait_recv()
        for d in range(1, slabs):
            source = lax.rem(me + slabs - d, slabs)
            total = total + stat[step, source]
        for copy in sends:
            copy.wait_send()
        mean = jnp.sum(total, keepdims=True) / (depth_total * pixels)
        factor = scale * lax.rsqrt(mean + NORM_GUARD)
        xs[:ext] = xs[:ext] - factor * grad[...]

    def sart(frame, n):
        x = xs[:ext]
        xb = x.astype(jnp.bfloat16)
        centre = jnp.sum(x, axis=1, keepdims=True) * (1.0 / pixels)
        width = 256
        for lo in range(0, pixels, width):
            lanes = slice(lo, lo + width)
            y = jnp.dot(
                xb, gram[n * pixels : (n + 1) * pixels, lanes], preferred_element_type=jnp.float32
            )
            y = y + centre * defect[n, 0:1, lanes]
            change = (back[frame, n, :, lanes] - y) * cover[n : n + 1, lanes]
            xs[:ext, lanes] = jnp.maximum(x[:, lanes] + change, 0.0)

    def sweep_body(sweep, carry):
        frame = lax.div(sweep, SWEEPS)
        for at in range(1, FRAMES):
            @pl.when(sweep == at * SWEEPS)
            def _():
                for copy in rim_copies(at):
                    copy.start()
                take_rims(at)
                for copy in edge_copies(at):
                    copy.wait_recv()

        for k in range(TV_STEPS):
            scale = jnp.float32(0.0)
            for s in range(SWEEPS):
                value = STEP_SCALE * STEP_DECAY ** (s * TV_STEPS + k)
                scale = jnp.where(lax.rem(sweep, SWEEPS) == s, jnp.float32(value), scale)
            tv_step(sweep * TV_STEPS + k, scale)
            if k == 0:
                @pl.when(sweep == 0)
                def _():
                    sum_gram()
                    sum_back(0)

        @pl.when(sweep == 0)
        def _():
            gather_gram()
            spread_edges(0)
            for t in range(1, FRAMES):
                for d in range(1, views):
                    part_copy(t, d).start()
            weigh()
            for copy in edge_copies(0):
                copy.wait_recv()

        for t in range(1, FRAMES):
            @pl.when(sweep == t * SWEEPS - 2)
            def _():
                sum_back(t)

            @pl.when(sweep == t * SWEEPS - 1)
            def _():
                spread_edges(t)

        for n in range(per_view):
            sart(frame, n)

        for t in range(FRAMES):
            @pl.when(sweep == (t + 1) * SWEEPS - 1)
            def _():
                out_ref[t] = xs[RIM : RIM + rows]
        return carry

    lax.fori_loop(0, FRAMES * SWEEPS, sweep_body, 0)

    for d in range(1, views):
        target = wrap(mine + d, views)
        cover_copy(d, d).wait_send()
        sum_copy(d).wait_send()
        view_copy(d, mine, target).wait_send()
        for t in range(FRAMES):
            part_copy(t, d).wait_send()
            full_copy(t, d, mine, target).wait_send()
    for d in range(views):
        for e in range(half):
            if e > 0:
                layer_copy(d, e, me, mate(e)).wait_send()
            pair_copy(d, e, mate(-e)).wait_send()
    for t in range(FRAMES):
        for copy in edge_copies(t):
            copy.wait_send()


def iterate(gram_part, back_part, cover_part, warm, slabs, gz, views):
    rows, pixels = warm.shape
    ext = rows + 2 * RIM
    steps = FRAMES * SWEEPS * TV_STEPS
    per_view = back_part.shape[1]
    piece = gram_part.shape[0] // views
    band = rows // views
    vmem = pl.BlockSpec(memory_space=pltpu.VMEM)
    dma = pltpu.SemaphoreType.DMA
    f32 = jnp.float32
    return pl.pallas_call(
        functools.partial(iterate_kernel, slabs, gz, views),
        out_shape=jax.ShapeDtypeStruct((FRAMES, rows, pixels), f32),
        in_specs=[vmem] * 4,
        out_specs=vmem,
        scratch_shapes=[
            pltpu.VMEM((per_view * pixels, pixels), jnp.bfloat16),
            pltpu.VMEM((views, piece, pixels), jnp.bfloat16),
            pltpu.VMEM((FRAMES, per_view, ext, pixels), f32),
            pltpu.VMEM((FRAMES, views, per_view, band, pixels), f32),
            pltpu.VMEM((views, 8, pixels), f32),
            pltpu.VMEM((8, pixels), f32),
            pltpu.VMEM((ext + 8, pixels), f32),
            pltpu.VMEM((ext, pixels), f32),
            pltpu.VMEM((ext + 8, pixels), f32),
            pltpu.VMEM((per_view, 8, pixels), f32),
            pltpu.VMEM((steps, 8, RY), f32),
            pltpu.VMEM((steps, slabs, 8, RY), f32),
            pltpu.VMEM((FRAMES, 2, RIM, pixels), f32),
            dma((views,)), dma((views,)), dma((views,)), dma((views,)), dma((views,)), dma((views,)),
            dma((views, slabs // 2)), dma((views, slabs // 2)),
            dma((views, slabs // 2)), dma((views, slabs // 2)),
            dma((FRAMES, views)), dma((FRAMES, views)), dma((FRAMES, views)), dma((FRAMES, views)),
            dma((FRAMES, 2)), dma((FRAMES, 2)),
            dma((steps, slabs)), dma((steps, slabs)),
            dma((FRAMES, 2)), dma((FRAMES, 2)),
        ],
        compiler_params=pltpu.CompilerParams(
            collective_id=0, has_side_effects=True, vmem_limit_bytes=40 * 2**20
        ),
    )(gram_part, back_part, cover_part, warm)


def body(tm, gz, views, sinogram, projector, warm_volume, view_order):
    slices, pixels = warm_volume.shape
    per_view = projector.shape[0]
    slabs = tm * gz
    slab = lax.axis_index("tm") * gz + lax.axis_index("gz")
    share = pixels // slabs
    ray_sums = jnp.sum(projector, axis=1, dtype=jnp.float32)
    cover = jnp.sum(projector, axis=2, dtype=jnp.float32)
    rays = 1.0 / ray_sums[:, None, :]
    part = lax.dynamic_slice_in_dim(projector, slab * share, share, axis=1)
    weighted = (part.astype(jnp.float32) * rays).astype(jnp.bfloat16)
    measured = (sinogram.astype(jnp.float32) * rays[None]).astype(jnp.bfloat16)
    measured = jnp.swapaxes(measured, 0, 1).reshape(per_view, FRAMES * slices, -1)
    left = jnp.concatenate([weighted, measured], axis=1)
    product = jnp.einsum("jmd,jpd->jmp", left, projector, preferred_element_type=jnp.float32)

    def ordered(block):
        return jnp.concatenate(
            [lax.dynamic_slice_in_dim(block, view_order[n], 1, axis=0) for n in range(per_view)],
            axis=0,
        )

    product = ordered(product)
    gram = product[:, :share].astype(jnp.bfloat16).reshape(per_view * share, pixels)
    back = jnp.swapaxes(product[:, share:].reshape(per_view, FRAMES, slices, pixels), 0, 1)
    cover = jnp.pad(ordered(cover), ((0, 8 - per_view), (0, 0)), constant_values=1.0)
    return iterate(gram, back, cover, warm_volume, slabs, gz, views)


def solution(mesh):
    return jax.shard_map(
        functools.partial(body, mesh.shape["tm"], mesh.shape["gz"], mesh.shape["view"]),
        mesh=mesh,
        in_specs=(
            P(None, "view", ("tm", "gz"), None),
            P("view", None, None),
            P(("tm", "gz"), None),
            P(),
        ),
        out_specs=P(None, ("tm", "gz"), None),
        check_vma=False,
    )
```

time: 250 us -> 141 us (0.56)
  waiting for transfers between devices: 127 us -> 0 us
  Pallas kernels: 57.1 us -> 117 us
  local copies, waits for them, and re-layouts: 17.4 us -> 3.75 us
  between operations: 13.3 us -> 3.95 us
  blocking collectives: 8.28 us -> 0 us
  other arithmetic: 14.3 us -> 9.31 us
  starting transfers between devices: 4.09 us -> 0 us
    pallas_call x1, Pallas kernels: 57.1 us -> 117 us  [iterate(): pl.pallas_call(functools.partial(iterate_kernel, slabs, gz, views), out_s...]
    all_gather x1 -> x0, waiting for transfers between devices: 57.4 us -> none  [body(): lax.all_gather(gram.astype(jnp.bfloat16), ('tm', 'gz', 'view'), axis=1, t...]
    psum x1 -> x0, waiting for transfers between devices: 41.3 us -> none  [body(): lax.psum(product[:, share:], 'view')]
    reduce_scatter x1 -> x0, waiting for transfers between devices: 24.8 us -> none  [body(): lax.psum_scatter(product[:, :share], 'view', scatter_dimension=1, tiled=T...]
    gather x5 -> x0, local copies, waits for them, and re-layouts: 14.2 us -> none  [the longest x3 11.8 us: body(): gram = jnp.take(gram, view_order, axis=0)]
    psum x1 -> x0, blocking collectives: 8.28 us -> none  [body(): cover = lax.psum(jnp.sum(projector, axis=2, dtype=jnp.float32), 'view')]
    ppermute x4 -> x0, starting transfers between devices: 4.01 us -> none  [the longest x2 2.5 us: with_rims(): lax.ppermute(lax.slice_in_dim(block, block.shape[dim] - RIM, None, axis=d...]
    select_n x4 -> x0, other arithmetic: 3.26 us -> none  [the longest x2 2.98 us: body(): gram = jnp.take(gram, view_order, axis=0)]
  transfers between devices with their start and end apart: 7 -> 0, of which waited for: 5 -> 0; matrix products, arithmetic and copies ran while one was open for 2% -> 0% of each run, Pallas kernels for 0% -> 0%
where the time goes in v2:
time: 141 us; the launch traced here: 139 us
  Pallas kernels  117 us (83%)
  other arithmetic  9.31 us (7%)
  matrix products  4.61 us (3%)
  between operations  3.95 us (3%)
  local copies, waits for them, and re-layouts  3.75 us (3%)
    pallas_call x1, Pallas kernels, iterate(): pl.pallas_call(functools.partial(iterate_kernel, slabs, gz, views), out_s...  117 us
    reduce_sum x1, other arithmetic, body(): cover = jnp.sum(projector, axis=2, dtype=jnp.float32)  7.61 us
    dot_general x1, matrix products, body(): jnp.einsum('jmd,jpd->jmp', left, projector, preferred_element_type=jnp.fl...  4.61 us

profile of v2, /device:TPU:25, one launch (start us, length us, event | category | flops | bytes accessed | tf_op | source)
XLA Modules:
  0.0 138.9 jit_solution(6736771529282053177)
XLA Ops:
  0.0 0.0 copy-start.1
  0.0 7.6 %convert_reduce_fusion = (f32[2,1024]{1,0:T(2,128)S(1)}, f32[2,2560]{1,0:T(2,128)S(1)}) fusion(bf16[2,1024,2560]{2,1,0:T(8,128)(2,1)} %param.5), kind=kLoop, calls=%fused_computation | loop fusion | flops 15721472 | bytes 10514432 | tf_op jit(solution)/shard_map/reduce_sum | solution.py:427
  7.6 0.0 copy-start.2
  7.7 0.0 copy-done.1
  7.7 1.3 multiply_convert_fusion.1
  9.0 0.2 copy-done.2
  9.2 0.2 fusion.4
  9.4 1.2 copy.6
  10.6 0.0 copy-start.3
  10.6 4.6 %fusion = f32[2,256,1024]{2,1,0:T(8,128)S(1)} fusion(bf16[2,1024,2560]{2,1,0:T(8,128)(2,1)S(1)} %copy-done.1, bf16[2,128,2560]{2,1,0:T(8,128)(2,1)} %bitcast.14, bf16[2,128,2560]{2,1,0:T(8,128)(2,1)} %multiply_convert_fusion.1), kind=kOutput, calls=%fused_computation.2 | convolution fusion | flops 2689597440 | bytes 15204352 | tf_op jit(solution)/shard_map/jmd,jpd->jmp/dot_general | solution.py:434
  15.2 0.0 copy-done.3
  15.2 0.6 fusion.8
  19.6 0.1 constant_dynamic-slice_fusion.2
  19.8 0.1 pad_maximum_fusion
  19.9 0.0 copy-start
  19.9 0.1 copy.9
  20.0 0.1 fusion.6
  20.1 0.7 copy-done
  20.8 117.3 %shard_map.46 = f32[2,64,1024]{2,1,0:T(8,128)S(1)} custom-call(bf16[256,1024]{1,0:T(8,128)(2,1)S(1)} %bitcast.12, f32[2,2,64,1024]{3,2,1,0:T(8,128)S(1)} %bitcast.11, f32[8,1024]{1,0:T(8,128)S(1)} %select_maximum_fusion.cover_part, f32[64,1024]{1,0:T(8,128)S(1)} %copy-done), custom_call_target="tpu_custom_call" | custom-call | tf_op jit(solution)/shard_map/pallas_call | solution.py:387
  138.1 0.8 copy.11
  (3 shorter events, 0.0 us)
Async XLA Ops:
  0.0 7.7 %copy-start.1 = (bf16[2,1024,2560]{2,1,0:T(8,128)(2,1)S(1)}, bf16[2,1024,2560]{2,1,0:T(8,128)(2,1)}, u32[]{:S(2)}) copy-start(bf16[2,1024,2560]{2,1,0:T(8,128)(2,1)} %param.5) | copy-start | bytes 31457284
  7.6 1.6 %copy-start.2 = (bf16[2,2,64,2560]{3,2,1,0:T(8,128)(2,1)S(1)}, bf16[2,2,64,2560]{3,2,1,0:T(8,128)(2,1)}, u32[]{:S(2)}) copy-start(bf16[2,2,64,2560]{3,2,1,0:T(8,128)(2,1)} %param.4) | copy-start | bytes 3932164
  10.6 4.6 %copy-start.3 = (s32[2]{0:T(128)S(1)}, s32[2]{0:T(128)}, u32[]{:S(2)}) copy-start(s32[2]{0:T(128)} %param.7) | copy-start | bytes 28
  19.9 1.0 copy-start

commit v3 on v2

--- a/solution.py
+++ b/solution.py
@@ -169,6 +169,8 @@
         for e in range(1, half):
             layer_copy(0, e, me, mate(e)).start()
         pair_copy(0, 0, me).start()
+        for d in range(1, views):
+            part_copy(0, d).start()
 
     def gather_gram():
         for d in range(1, views):
@@ -176,6 +178,7 @@
             for e in range(1, half):
                 layer_copy(d, e, me, mate(e)).start()
             pair_copy(d, 0, me).start()
+        sum_back(0)
         for d in range(views):
             for e in range(1, half):
                 layer_copy(d, e, mate(-e), mate(-e)).wait_recv()
@@ -222,8 +225,6 @@
         sum_copy(d).start()
     for d in range(1, views):
         cover_copy(d, d).start()
-    for d in range(1, views):
-        part_copy(0, d).start()
     take_rims(0)
 
     def tv_step(step, scale):
@@ -323,7 +324,6 @@
                 @pl.when(sweep == 0)
                 def _():
                     sum_gram()
-                    sum_back(0)
 
         @pl.when(sweep == 0)
         def _():
@@ -424,13 +424,14 @@
     slab = lax.axis_index("tm") * gz + lax.axis_index("gz")
     share = pixels // slabs
     ray_sums = jnp.sum(projector, axis=1, dtype=jnp.float32)
-    cover = jnp.sum(projector, axis=2, dtype=jnp.float32)
     rays = 1.0 / ray_sums[:, None, :]
     part = lax.dynamic_slice_in_dim(projector, slab * share, share, axis=1)
     weighted = (part.astype(jnp.float32) * rays).astype(jnp.bfloat16)
     measured = (sinogram.astype(jnp.float32) * rays[None]).astype(jnp.bfloat16)
     measured = jnp.swapaxes(measured, 0, 1).reshape(per_view, FRAMES * slices, -1)
-    left = jnp.concatenate([weighted, measured], axis=1)
+    left = jnp.concatenate(
+        [weighted, measured, jnp.ones((per_view, 8, projector.shape[2]), jnp.bfloat16)], axis=1
+    )
     product = jnp.einsum("jmd,jpd->jmp", left, projector, preferred_element_type=jnp.float32)
 
     def ordered(block):
@@ -440,9 +441,10 @@
         )
 
     product = ordered(product)
+    filled = share + FRAMES * slices
     gram = product[:, :share].astype(jnp.bfloat16).reshape(per_view * share, pixels)
-    back = jnp.swapaxes(product[:, share:].reshape(per_view, FRAMES, slices, pixels), 0, 1)
-    cover = jnp.pad(ordered(cover), ((0, 8 - per_view), (0, 0)), constant_values=1.0)
+    back = jnp.swapaxes(product[:, share:filled].reshape(per_view, FRAMES, slices, pixels), 0, 1)
+    cover = jnp.pad(product[:, filled], ((0, 8 - per_view), (0, 0)), constant_values=1.0)
     return iterate(gram, back, cover, warm_volume, slabs, gz, views)
 
 

time: 141 us -> 134 us (0.950); the launches traced: 139 us -> 134 us
  Pallas kernels: 117 us -> 109 us
  local copies, waits for them, and re-layouts: 3.75 us -> 6.44 us
    pallas_call x1, Pallas kernels: 117 us -> 109 us  [iterate(): pl.pallas_call(functools.partial(iterate_kernel, slabs, gz, views), out_s...]
    unnamed x9 -> x11, local copies, waits for them, and re-layouts: 1.75 us -> 4.07 us
    reduce_sum x1, other arithmetic: 7.61 us -> 5.88 us  [body(): ray_sums = jnp.sum(projector, axis=1, dtype=jnp.float32)]
where the time goes in v3:
time: 134 us
  Pallas kernels  109 us (81%)
  other arithmetic  9.32 us (7%)
  local copies, waits for them, and re-layouts  6.44 us (5%)
  matrix products  4.71 us (4%)
  between operations  3.91 us (3%)
    pallas_call x1, Pallas kernels, iterate(): pl.pallas_call(functools.partial(iterate_kernel, slabs, gz, views), out_s...  109 us
    reduce_sum x1, other arithmetic, body(): ray_sums = jnp.sum(projector, axis=1, dtype=jnp.float32)  5.88 us
    dot_general x1, matrix products, body(): jnp.einsum('jmd,jpd->jmp', left, projector, preferred_element_type=jnp.fl...  4.71 us
    unnamed x11, local copies, waits for them, and re-layouts  4.07 us

profile of v3, /device:TPU:25, one launch (start us, length us, event | category | flops | bytes accessed | tf_op | source)
XLA Modules:
  0.0 133.7 jit_solution(18283142919438242084)
XLA Ops:
  0.0 0.0 copy-start.1
  0.0 5.9 %convert_reduce_fusion = f32[2,2560]{1,0:T(2,128)S(1)} fusion(bf16[2,1024,2560]{2,1,0:T(8,128)(2,1)} %param.5), kind=kLoop, calls=%fused_computation | loop fusion | flops 10480640 | bytes 10506240 | tf_op jit(solution)/shard_map/reduce_sum | solution.py:426
  5.9 0.0 copy-start.2
  5.9 1.0 copy-done.1
  7.0 1.3 multiply_convert_fusion.1
  8.3 0.0 copy-done.2
  8.3 0.2 fusion.6
  8.5 1.2 copy.9
  9.6 0.0 copy-start.3
  9.7 4.7 %fusion = f32[2,264,1024]{2,1,0:T(8,128)S(1)} fusion(bf16[2,1024,2560]{2,1,0:T(8,128)(2,1)S(1)} %copy-done.1, bf16[2,128,2560]{2,1,0:T(8,128)(2,1)} %bitcast.16, bf16[2,128,2560]{2,1,0:T(8,128)(2,1)} %multiply_convert_fusion.1, bf16[264]{0:T(512)(128)(2,1)S(1)} %pad.9.clone), kind=kOutput, calls=%fused_computation.1 | convolution fusion | flops 2776350720 | bytes 15270416 | tf_op jit(solution)/shard_map/jmd,jpd->jmp/dot_general | solution.py:435
  14.4 0.0 copy-done.3
  14.4 0.6 fusion.12
  18.8 0.1 constant_dynamic-slice_fusion.1
  18.9 1.1 copy.14
  20.0 1.1 copy.15
  21.2 0.9 fusion.7
  22.2 0.3 copy.17
  22.5 0.0 copy-start
  22.5 0.9 fusion.9
  23.4 0.1 copy.12
  23.6 0.0 copy-done
  23.6 109.3 %shard_map.46 = f32[2,64,1024]{2,1,0:T(8,128)S(1)} custom-call(bf16[256,1024]{1,0:T(8,128)(2,1)S(1)} %bitcast.14, f32[2,2,64,1024]{3,2,1,0:T(8,128)S(1)} %bitcast.13, f32[8,1024]{1,0:T(8,128)S(1)} %pad.4.cover_part, f32[64,1024]{1,0:T(8,128)S(1)} %copy-done), custom_call_target="tpu_custom_call" | custom-call | tf_op jit(solution)/shard_map/pallas_call | solution.py:387
  132.9 0.8 copy.19
  (5 shorter events, 0.1 us)
Async XLA Ops:
  0.0 7.0 %copy-start.1 = (bf16[2,1024,2560]{2,1,0:T(8,128)(2,1)S(1)}, bf16[2,1024,2560]{2,1,0:T(8,128)(2,1)}, u32[]{:S(2)}) copy-start(bf16[2,1024,2560]{2,1,0:T(8,128)(2,1)} %param.5) | copy-start | bytes 31457284
  5.9 2.4 %copy-start.2 = (bf16[2,2,64,2560]{3,2,1,0:T(8,128)(2,1)S(1)}, bf16[2,2,64,2560]{3,2,1,0:T(8,128)(2,1)}, u32[]{:S(2)}) copy-start(bf16[2,2,64,2560]{3,2,1,0:T(8,128)(2,1)} %param.4) | copy-start | bytes 3932164
  9.6 4.7 %copy-start.3 = (s32[2]{0:T(128)S(1)}, s32[2]{0:T(128)}, u32[]{:S(2)}) copy-start(s32[2]{0:T(128)} %param.7) | copy-start | bytes 28
  22.5 1.1 copy-start

commit v4 on v3

--- a/solution.py
+++ b/solution.py
@@ -417,34 +417,82 @@
     )(gram_part, back_part, cover_part, warm)
 
 
+def product_kernel(scalars, tile_ref, measured_ref, gram_ref, back_ref, cover_ref, total):
+    per_view = scalars.shape[0] - 1
+    share = gram_ref.shape[1]
+    rows = measured_ref.shape[2]
+    pixels, width = tile_ref.shape[1:]
+    tile = tile_ref[0]
+    ones = jnp.ones((16, pixels), jnp.bfloat16)
+    rays = 1.0 / jnp.dot(ones, tile, preferred_element_type=jnp.float32)[0:1]
+    first = pl.multiple_of(scalars[per_view] * share, 16)
+    parts = [tile_ref[0, pl.ds(first, share), :]]
+    parts += [measured_ref[t, 0] for t in range(FRAMES)]
+    left = jnp.concatenate(
+        [(part.astype(jnp.float32) * rays).astype(jnp.bfloat16) for part in parts]
+        + [jnp.ones((16, width), jnp.bfloat16)],
+        axis=0,
+    )
+    step = pl.program_id(1)
+
+    @pl.when(step == 0)
+    def _():
+        total[...] = jnp.zeros_like(total)
+
+    total[...] += lax.dot_general(
+        left, tile, (((1,), (1,)), ((), ())), preferred_element_type=jnp.float32
+    )
+
+    @pl.when(step == pl.num_programs(1) - 1)
+    def _():
+        gram_ref[0] = total[:share].astype(jnp.bfloat16)
+        for t in range(FRAMES):
+            back_ref[t, 0] = total[share + t * rows : share + (t + 1) * rows]
+        cover_ref[0] = total[share + FRAMES * rows :][:8]
+
+
+def products(scalars, projector, sinogram, slabs):
+    per_view, pixels, bins = projector.shape
+    rows = sinogram.shape[2]
+    share = pixels // slabs
+    width = 512 if bins % 512 == 0 else bins
+    f32 = jnp.float32
+    return pl.pallas_call(
+        product_kernel,
+        grid_spec=pltpu.PrefetchScalarGridSpec(
+            num_scalar_prefetch=1,
+            grid=(per_view, bins // width),
+            in_specs=[
+                pl.BlockSpec((1, pixels, width), lambda n, d, order: (order[n], 0, d)),
+                pl.BlockSpec((FRAMES, 1, rows, width), lambda n, d, order: (0, order[n], 0, d)),
+            ],
+            out_specs=[
+                pl.BlockSpec((1, share, pixels), lambda n, d, order: (n, 0, 0)),
+                pl.BlockSpec((FRAMES, 1, rows, pixels), lambda n, d, order: (0, n, 0, 0)),
+                pl.BlockSpec((1, 8, pixels), lambda n, d, order: (n, 0, 0)),
+            ],
+            scratch_shapes=[pltpu.VMEM((share + FRAMES * rows + 16, pixels), f32)],
+        ),
+        out_shape=[
+            jax.ShapeDtypeStruct((per_view, share, pixels), jnp.bfloat16),
+            jax.ShapeDtypeStruct((FRAMES, per_view, rows, pixels), f32),
+            jax.ShapeDtypeStruct((per_view, 8, pixels), f32),
+        ],
+        compiler_params=pltpu.CompilerParams(
+            dimension_semantics=("arbitrary", "arbitrary"), vmem_limit_bytes=32 * 2**20
+        ),
+    )(scalars, projector, sinogram)
+
+
 def body(tm, gz, views, sinogram, projector, warm_volume, view_order):
     slices, pixels = warm_volume.shape
     per_view = projector.shape[0]
     slabs = tm * gz
     slab = lax.axis_index("tm") * gz + lax.axis_index("gz")
-    share = pixels // slabs
-    ray_sums = jnp.sum(projector, axis=1, dtype=jnp.float32)
-    rays = 1.0 / ray_sums[:, None, :]
-    part = lax.dynamic_slice_in_dim(projector, slab * share, share, axis=1)
-    weighted = (part.astype(jnp.float32) * rays).astype(jnp.bfloat16)
-    measured = (sinogram.astype(jnp.float32) * rays[None]).astype(jnp.bfloat16)
-    measured = jnp.swapaxes(measured, 0, 1).reshape(per_view, FRAMES * slices, -1)
-    left = jnp.concatenate(
-        [weighted, measured, jnp.ones((per_view, 8, projector.shape[2]), jnp.bfloat16)], axis=1
-    )
-    product = jnp.einsum("jmd,jpd->jmp", left, projector, preferred_element_type=jnp.float32)
-
-    def ordered(block):
-        return jnp.concatenate(
-            [lax.dynamic_slice_in_dim(block, view_order[n], 1, axis=0) for n in range(per_view)],
-            axis=0,
-        )
-
-    product = ordered(product)
-    filled = share + FRAMES * slices
-    gram = product[:, :share].astype(jnp.bfloat16).reshape(per_view * share, pixels)
-    back = jnp.swapaxes(product[:, share:filled].reshape(per_view, FRAMES, slices, pixels), 0, 1)
-    cover = jnp.pad(product[:, filled], ((0, 8 - per_view), (0, 0)), constant_values=1.0)
+    scalars = jnp.concatenate([view_order, slab.reshape(1).astype(jnp.int32)])
+    gram, back, cover = products(scalars, projector, sinogram, slabs)
+    gram = gram.reshape(per_view * (pixels // slabs), pixels)
+    cover = jnp.pad(cover[:, 0], ((0, 8 - per_view), (0, 0)), constant_values=1.0)
     return iterate(gram, back, cover, warm_volume, slabs, gz, views)
 
 

time: 134 us -> 126 us (0.940)
  Pallas kernels: 109 us -> 119 us
  other arithmetic: 9.32 us -> 0.73 us
  matrix products: 4.71 us -> 0 us
  between operations: 3.91 us -> 0.05 us
    pallas_call x0 -> x1, Pallas kernels: none -> 9.9 us  [products(): pl.pallas_call(product_kernel, grid_spec=pltpu.PrefetchScalarGridSpec(num...]
    reduce_sum x1 -> x0, other arithmetic: 5.88 us -> none  [body(): ray_sums = jnp.sum(projector, axis=1, dtype=jnp.float32)]
    dot_general x1 -> x0, matrix products: 4.71 us -> none  [body(): jnp.einsum('jmd,jpd->jmp', left, projector, preferred_element_type=jnp.fl...]
    unnamed x11 -> x7, local copies, waits for them, and re-layouts: 4.07 us -> 6.11 us
where the time goes in v4:
time: 126 us
  Pallas kernels  119 us (94%)
  local copies, waits for them, and re-layouts  6.18 us (5%)
    pallas_call x1, Pallas kernels, iterate(): pl.pallas_call(functools.partial(iterate_kernel, slabs, gz, views), out_s...  109 us
    pallas_call x1, Pallas kernels, products(): pl.pallas_call(product_kernel, grid_spec=pltpu.PrefetchScalarGridSpec(num...  9.9 us
    unnamed x7, local copies, waits for them, and re-layouts  6.11 us

profile of v4, /device:TPU:25, one launch (start us, length us, event | category | flops | bytes accessed | tf_op | source)
XLA Modules:
  0.0 126.2 jit_solution(4418512326463939209)
XLA Ops:
  0.0 0.7 pad_add_fusion.scalars
  0.7 0.0 copy-start
  0.7 4.0 %copy-done = bf16[2,1024,2560]{2,1,0:T(8,128)(2,1)S(1)} copy-done((bf16[2,1024,2560]{2,1,0:T(8,128)(2,1)S(1)}, bf16[2,1024,2560]{2,1,0:T(8,128)(2,1)}, u32[]{:S(2)}) %copy-start) | copy-done | bytes 10485784
  4.7 0.0 copy-start.1
  4.7 1.3 %copy-done.1 = bf16[2,2,64,2560]{3,2,1,0:T(8,128)(2,1)S(1)} copy-done((bf16[2,2,64,2560]{3,2,1,0:T(8,128)(2,1)S(1)}, bf16[2,2,64,2560]{3,2,1,0:T(8,128)(2,1)}, u32[]{:S(2)}) %copy-start.1) | copy-done | bytes 1310744
  6.0 0.0 copy-start.2
  6.0 9.9 %shard_map.46 = (bf16[2,128,1024]{2,1,0:T(8,128)(2,1)S(1)}, f32[2,2,64,1024]{3,2,1,0:T(8,128)S(1)}, f32[2,8,1024]{2,1,0:T(8,128)S(1)}) custom-call(s32[3]{0:T(128)S(1)} %pad_add_fusion.scalars, bf16[2,1024,2560]{2,1,0:T(8,128)(2,1)S(1)} %copy-done, bf16[2,2,64,2560]{3,2,1,0:T(8,128)(2,1)S(1)} %copy-done.1), custom_call_target="tpu_custom_call" | custom-call | tf_op jit(solution)/shard_map/pallas_call | solution.py:460
  16.0 0.1 copy.5
  16.0 0.0 copy-done.2
  16.1 109.3 %shard_map.47 = f32[2,64,1024]{2,1,0:T(8,128)S(1)} custom-call(bf16[256,1024]{1,0:T(8,128)(2,1)S(1)} %bitcast.4, f32[2,2,64,1024]{3,2,1,0:T(8,128)S(1)} %get-tuple-element.9.back_part, f32[8,1024]{1,0:T(8,128)S(1)} %pad.4.cover_part, f32[64,1024]{1,0:T(8,128)S(1)} %copy-done.2), custom_call_target="tpu_custom_call" | custom-call | tf_op jit(solution)/shard_map/pallas_call | solution.py:387
  125.4 0.8 copy.7
  (2 shorter events, 0.0 us)
Async XLA Ops:
  0.7 4.0 %copy-start = (bf16[2,1024,2560]{2,1,0:T(8,128)(2,1)S(1)}, bf16[2,1024,2560]{2,1,0:T(8,128)(2,1)}, u32[]{:S(2)}) copy-start(bf16[2,1024,2560]{2,1,0:T(8,128)(2,1)} %tile_ref.1) | copy-start | bytes 31457284
  4.7 1.3 %copy-start.1 = (bf16[2,2,64,2560]{3,2,1,0:T(8,128)(2,1)S(1)}, bf16[2,2,64,2560]{3,2,1,0:T(8,128)(2,1)}, u32[]{:S(2)}) copy-start(bf16[2,2,64,2560]{3,2,1,0:T(8,128)(2,1)} %measured_ref.1) | copy-start | bytes 3932164
  6.0 10.0 %copy-start.2 = (f32[64,1024]{1,0:T(8,128)S(1)}, f32[64,1024]{1,0:T(8,128)}, u32[]{:S(2)}) copy-start(f32[64,1024]{1,0:T(8,128)} %warm_ref.1) | copy-start | bytes 786436

commit v5 on v4

--- a/solution.py
+++ b/solution.py
@@ -479,7 +479,7 @@
             jax.ShapeDtypeStruct((per_view, 8, pixels), f32),
         ],
         compiler_params=pltpu.CompilerParams(
-            dimension_semantics=("arbitrary", "arbitrary"), vmem_limit_bytes=32 * 2**20
+            dimension_semantics=("arbitrary", "arbitrary"), vmem_limit_bytes=58 * 2**20
         ),
     )(scalars, projector, sinogram)
 

time: 126 us -> 128 us (1.016)
  Pallas kernels: 119 us -> 123 us
  local copies, waits for them, and re-layouts: 6.18 us -> 3.96 us
    pallas_call x1, Pallas kernels: 9.9 us -> 13.4 us  [products(): pl.pallas_call(product_kernel, grid_spec=pltpu.PrefetchScalarGridSpec(num...]
    unnamed x7, local copies, waits for them, and re-layouts: 6.11 us -> 3.06 us
where the time goes in v5:
time: 128 us
  Pallas kernels  123 us (96%)
  local copies, waits for them, and re-layouts  3.96 us (3%)
  other arithmetic  1.34 us (1%)
    pallas_call x1, Pallas kernels, iterate(): pl.pallas_call(functools.partial(iterate_kernel, slabs, gz, views), out_s...  109 us
    pallas_call x1, Pallas kernels, products(): pl.pallas_call(product_kernel, grid_spec=pltpu.PrefetchScalarGridSpec(num...  13.4 us
    unnamed x7, local copies, waits for them, and re-layouts  3.06 us

profile of v5, /device:TPU:25, one launch (start us, length us, event | category | flops | bytes accessed | tf_op | source)
XLA Modules:
  0.0 128.0 jit_solution(3357279671872424878)
XLA Ops:
  0.0 0.0 copy-start.2
  0.0 1.3 %pad_add_fusion.scalars = s32[3]{0:T(128)} fusion(s32[1]{0:T(128)} %bitcast, s32[2]{0:T(128)} %param.7), kind=kLoop, calls=%fused_computation.1 | loop fusion | flops 3 | bytes 24 | tf_op jit(solution)/shard_map/concatenate | solution.py:492
  1.3 13.4 %shard_map.46 = (bf16[2,128,1024]{2,1,0:T(8,128)(2,1)}, f32[2,2,64,1024]{3,2,1,0:T(8,128)}, f32[2,8,1024]{2,1,0:T(8,128)}) custom-call(s32[3]{0:T(128)} %pad_add_fusion.scalars, bf16[2,1024,2560]{2,1,0:T(8,128)(2,1)} %tile_ref.1, bf16[2,2,64,2560]{3,2,1,0:T(8,128)(2,1)} %measured_ref.1), custom_call_target="tpu_custom_call" | custom-call | tf_op jit(solution)/shard_map/pallas_call | solution.py:460
  14.7 0.9 copy.5
  15.6 0.0 copy-done.2
  15.6 0.0 copy-start
  15.6 1.2 copy-done
  16.9 0.0 copy-start.1
  16.9 1.0 copy-done.1
  17.9 109.3 %shard_map.47 = f32[2,64,1024]{2,1,0:T(8,128)S(1)} custom-call(bf16[256,1024]{1,0:T(8,128)(2,1)S(1)} %bitcast.4, f32[2,2,64,1024]{3,2,1,0:T(8,128)S(1)} %copy-done, f32[8,1024]{1,0:T(8,128)S(1)} %pad.4.cover_part, f32[64,1024]{1,0:T(8,128)S(1)} %copy-done.2), custom_call_target="tpu_custom_call" | custom-call | tf_op jit(solution)/shard_map/pallas_call | solution.py:387
  127.2 0.8 copy.7
  (2 shorter events, 0.0 us)
Async XLA Ops:
  0.0 15.6 %copy-start.2 = (f32[64,1024]{1,0:T(8,128)S(1)}, f32[64,1024]{1,0:T(8,128)}, u32[]{:S(2)}) copy-start(f32[64,1024]{1,0:T(8,128)} %warm_ref.1) | copy-start | bytes 786436
  15.6 1.2 copy-start
  16.9 1.0 copy-start.1
